TPU v7x, 256 devices: a whole 4x4x8 slice. The times are simulated.
256 devices in a mesh: row: 16 (over y, z_hi), col: 16 (over z_lo, x, core).
Axes of the slice: x: 4, y: 4, z: 8 (z_hi: 4, z_lo: 2; z = z_hi * 2 + z_lo), core: 2. Of those that a mesh axis runs over, the one named last changes fastest.
Arguments:
- fields: float32 [2, 1024, 2048, 128], P(None, 'row', 'col'), may hold values from -6 to 6
- factor_one: float32 [1024, 32], P('row'), may hold values from -0.1875 to 0.1875
- factor_two: float32 [2048, 32], P('col'), may hold values from -0.125 to 0.125
- factor_three: float32 [128, 32], replicated, may hold values from -0.5 to 0.5
Outputs:
- core: float32 [2, 32, 32, 32], replicated
- gram_one: float32 [2, 1024, 1024], P(None, 'row', 'col')
- gram_two: float32 [2, 2048, 2048], P(None, 'col', 'row')
All inputs are finite; a program needn't handle non-finite values.
Results may differ from a plain program's by a relative error of at most 0.000076.
Values sent between devices are 32-bit elements; how exact they have to be, the bound alone decides.
A program may use at most 64 MiB of HBM per device.

v0:
```python
import functools

import jax
import jax.numpy as jnp
from jax import lax
from jax.experimental import pallas as pl
from jax.experimental.pallas import tpu as pltpu
from jax.sharding import PartitionSpec as P

F32 = jnp.float32
BF16 = jnp.bfloat16
MESH = pl.DeviceIdType.MESH
RANK = 32
CHUNKS = 4


def split(x):
    high = x.astype(BF16)
    return high, (x - high.astype(F32)).astype(BF16)


def dot(a, b, dims):
    return lax.dot_general(a, b, ((dims[0], dims[1]), ((), ())), preferred_element_type=F32)


def stack_factor(f):
    high, low = split(f)
    return jnp.concatenate([jnp.concatenate([high, high], 1), jnp.concatenate([low, low], 1)], 0)


def kernel(
    fields, factors, core_out, g1_out, g2_out,
    xbuf, p3, p2, p1, wcore,
    ry1, ryf, rz1, rzf, rc1, rc2,
    p2c, p1t, p2r, p1r, cy, cz, cc,
    xsem, ss, rs,
):
    r, c = lax.axis_index("row"), lax.axis_index("col")
    y, h = r // 4, r % 4
    l, x, co = c // 8, (c // 2) % 4, c % 2

    def ring(v, d):
        return (v + d) % 4

    def at_y(d):
        return (ring(y, d) * 4 + h, c)

    def at_h(d):
        return (y * 4 + ring(h, d), c)

    def at_x(d):
        return (r, l * 8 + ring(x, d) * 2 + co)

    at_l = (r, (1 - l) * 8 + x * 2 + co)
    at_co = (r, l * 8 + x * 2 + (1 - co))
    x_r = (r // 2) % 4
    at_t2 = (c, (h // 2) * 8 + ring(y, x) * 2 + h % 2)
    at_t1 = ((ring(x, 4 - x_r)) * 4 + l * 2 + co, r)
    away = jnp.logical_or(at_t2[0] != r, at_t2[1] != c)

    def load(i):
        return pltpu.make_async_copy(fields.at[i // 2, pl.ds(i % 2 * 32, 32)], xbuf.at[i], xsem.at[i])

    for i in range(CHUNKS):
        load(i).start()
    barrier = pltpu.get_barrier_semaphore()
    def at_lx(d):
        return (r, (1 - l) * 8 + ring(x, d) * 2 + co)

    partners = [at(d) for at in (at_y, at_h, at_x, at_lx) for d in (1, 2, 3)] + [at_l, at_co]
    for to in partners:
        pl.semaphore_signal(barrier, inc=1, device_id=to, device_id_type=MESH)

    @pl.when(away)
    def _():
        pl.semaphore_signal(barrier, inc=1, device_id=at_t1, device_id_type=MESH)
        pl.semaphore_signal(barrier, inc=1, device_id=at_t2, device_id_type=MESH)

    sent = []

    def copy(idx, src, dst, to):
        return pltpu.make_async_remote_copy(
            src_ref=src, dst_ref=dst, send_sem=ss.at[idx], recv_sem=rs.at[idx], device_id=to, device_id_type=MESH
        )

    counter = [0]

    def new(n=1):
        counter[0] += n
        return counter[0] - n

    def send(idx, src, dst, to):
        copy(idx, src, dst, to).start()
        sent.append((idx, src))

    def arrived(idx, dst):
        copy(idx, dst, dst, at_co).wait_recv()

    f3, f1, f2 = factors[:, :128], factors[:, 256:320], factors[:, 128:256]
    l3, l1, l2 = stack_factor(f3), stack_factor(f1), stack_factor(f2)
    wcore[...] = jnp.zeros_like(wcore)
    for b in range(4):
        wcore[pl.ds(b * 32, 32), pl.ds(b * 64, 64)] = f1

    def project(i, _):
        load(i).wait()
        for n in range(16):
            high, low = split(xbuf[i, pl.ds(n * 2, 2)].reshape(256, 128))
            out = dot(l3, jnp.concatenate([high, low], 1), ((1,), (1,)))
            out = out[:RANK] + out[RANK:]
            at = pl.multiple_of(i * 32 * RANK, RANK) + n * 2 * RANK
            p3[pl.ds(at, RANK), :] = out[:, :128]
            p3[pl.ds(at + RANK, RANK), :] = out[:, 128:]
        return 0

    lax.fori_loop(0, CHUNKS, project, 0)

    def mode_two(ys, hs):
        k = ys * 4 + hs
        right = []
        for half in range(2):
            hi, lo = split(p3[pl.ds(k + 16 * half, 128, stride=RANK), :])
            right.extend(jnp.concatenate([hi[s * 64:s * 64 + 64], lo[s * 64:s * 64 + 64]], 0) for s in range(2))
        out = dot(l1, jnp.concatenate(right, 1), ((1,), (0,)))
        out = out[:RANK] + out[RANK:]
        for half in range(2):
            for s in range(2):
                at = half * 256 + s * 128
                p2[ys, hs, s, pl.ds(half * RANK, RANK), :] = out[:, at:at + 128]

    def mode_one(k):
        parts = [jnp.concatenate(split(p3[pl.ds(half * 16 + k, 128, stride=RANK), :]), 1) for half in range(2)]
        out = dot(l2, jnp.concatenate(parts, 0), ((1,), (1,)))
        out = out[:RANK] + out[RANK:]
        for half in range(2):
            p1[k // 8, (k // 2) % 4, k % 2, pl.ds(half * RANK, RANK), :] = out[:, half * 128:half * 128 + 128]

    pl.semaphore_wait(barrier, len(partners) + jnp.where(away, 2, 0))

    order = (2, 1, 3, 0)
    m_y1 = [new(4), new(4)]
    m_yf = {(side, s): new(4) for side in range(2) for s in range(2)}

    m_core, m_x = new(), new(8)
    for k in range(16):
        mode_one(k)
    send(m_core, p1.at[:, :, 1 - co], rc1, at_co)
    for dy in order:
        if dy == 3:
            arrived(m_core, rc1)
            for lk in range(2):
                for xk in range(4):
                    p1[lk, xk, co] += rc1[lk, xk]
            for d in (2, 1, 3):
                send(m_x + d, p1.at[l, ring(x, d), co], rc2.at[d], at_x(d))
                send(m_x + 4 + d, p1.at[1 - l, ring(x, d), co], rc2.at[4 + d], at_lx(d))
            send(m_x + 4, p1.at[1 - l, x, co], rc2.at[4], at_l)
        for n, dh in enumerate(order):
            ys, hs = ring(y, dy), ring(h, dh)
            mode_two(ys, hs)
            if dy == 2:
                send(m_y1[0] + n, p2.at[ys, hs, 0], ry1.at[0, hs], at_y(1))
                send(m_y1[1] + n, p2.at[ys, hs, 1], ry1.at[1, hs], at_y(3))

    def y_late(n):
        hs = ring(h, order[n])
        up, down = ring(y, 1), ring(y, 3)
        send(m_yf[0, 1] + n, p2.at[up, hs, 1], ryf.at[0, hs, 1], at_y(1))
        send(m_yf[1, 0] + n, p2.at[down, hs, 0], ryf.at[1, hs, 0], at_y(3))
        arrived(m_y1[0] + n, ry1.at[0, hs])
        p2[up, hs, 0] += ry1[0, hs]
        send(m_yf[0, 0] + n, p2.at[up, hs, 0], ryf.at[0, hs, 0], at_y(1))
        arrived(m_y1[1] + n, ry1.at[1, hs])
        p2[down, hs, 1] += ry1[1, hs]
        send(m_yf[1, 1] + n, p2.at[down, hs, 1], ryf.at[1, hs, 1], at_y(3))

    def y_final(n):
        hs = ring(h, order[n])
        for s in (1, 0):
            for side in range(2):
                arrived(m_yf[side, s] + n, ryf.at[side, hs, s])
            p2[y, hs, s] += ryf[0, hs, s] + ryf[1, hs, s]

    def gather_row(buf):
        mz = new(6)
        my = [new(4) for _ in range(4)]

        def to_y(dh):
            mine = buf.at[y, ring(h, dh)]
            send(my[dh], mine, mine, at_y(1))
            send(my[dh] + 1, mine, mine, at_y(3))

        def y_step(dh):
            hs = ring(h, dh)
            got = buf.at[ring(y, 3), hs]
            arrived(my[dh], got)
            send(my[dh] + 2, got.at[0], got.at[0], at_y(1))
            got = buf.at[ring(y, 1), hs]
            arrived(my[dh] + 1, got)
            send(my[dh] + 3, got.at[1], got.at[1], at_y(3))

        mine = buf.at[y, h]
        for half in range(2):
            send(mz + 4 * half, mine.at[half], mine.at[half], at_h(1))
            send(mz + 1 + 4 * half, mine.at[1 - half], mine.at[1 - half], at_h(3))
        to_y(0)
        yield
        y_step(0)
        yield
        below, above = buf.at[y, ring(h, 3)], buf.at[y, ring(h, 1)]
        arrived(mz, below.at[0])
        send(mz + 2, below.at[0], below.at[0], at_h(1))
        arrived(mz + 1, above.at[1])
        send(mz + 3, above.at[1], above.at[1], at_h(3))
        arrived(mz + 4, below.at[1])
        to_y(3)
        arrived(mz + 5, above.at[0])
        to_y(1)
        yield
        got = buf.at[y, ring(h, 2)]
        arrived(mz + 2, got.at[0])
        arrived(mz + 3, got.at[1])
        to_y(2)
        yield
        y_step(3)
        y_step(1)
        yield
        y_step(2)
        yield
        for dh in (0, 3, 1, 2):
            got = buf.at[ring(y, 2), ring(h, dh)]
            arrived(my[dh] + 2, got.at[0])
            arrived(my[dh] + 3, got.at[1])
        yield

    def gather_col(buf):
        ml = new()
        mx = [new(4), new(4)]
        mc = new(8)

        def to_x(lk, k):
            mine = buf.at[lk, x, co]
            send(mx[k], mine, mine, at_x(1))
            send(mx[k] + 1, mine, mine, at_x(3))
            if k:
                send(mx[k] + 2, mine, mine, at_x(2))

        def to_co(lk, k, dx):
            mine = buf.at[lk, ring(x, dx), co]
            send(mc + k * 4 + dx, mine, mine, at_co)

        def x_step(lk, k):
            got = buf.at[lk, ring(x, 3), co]
            arrived(mx[k], got)
            if not k:
                send(mx[k] + 2, got.at[0], got.at[0], at_x(1))
            to_co(lk, k, 3)
            got = buf.at[lk, ring(x, 1), co]
            arrived(mx[k] + 1, got)
            if not k:
                send(mx[k] + 3, got.at[1], got.at[1], at_x(3))
            to_co(lk, k, 1)

        mine = buf.at[l, x, co]
        send(ml, mine, mine, at_l)
        to_x(l, 0)
        to_co(l, 0, 0)
        yield
        arrived(ml, buf.at[1 - l, x, co])
        to_x(1 - l, 1)
        to_co(1 - l, 1, 0)
        yield
        x_step(l, 0)
        yield
        x_step(1 - l, 1)
        yield
        for k, lk in enumerate((l, 1 - l)):
            got = buf.at[lk, ring(x, 2), co]
            if k:
                arrived(mx[k] + 2, got)
            else:
                arrived(mx[k] + 2, got.at[0])
                arrived(mx[k] + 3, got.at[1])
            to_co(lk, k, 2)
        yield
        for k, lk in enumerate((l, 1 - l)):
            for dx in range(4):
                arrived(mc + k * 4 + dx, buf.at[lk, ring(x, dx), 1 - co])
        yield

    for n in range(4):
        y_late(n)

    m_z1 = [new(), new()]
    m_zf = {(side, s): new() for side in range(2) for s in range(2)}
    y_final(0)
    send(m_z1[0], p2.at[y, ring(h, 2), 0], rz1.at[0], at_h(1))
    send(m_z1[1], p2.at[y, ring(h, 2), 1], rz1.at[1], at_h(3))
    piece = p1[l, x, co]
    for k in range(1, 8):
        arrived(m_x + k, rc2.at[k])
        piece = piece + rc2[k]
    p1r[l, x, co] = piece.reshape(2, RANK, 128)
    m_t1, m_t2 = new(), new()

    @pl.when(away)
    def _():
        copy(m_t1, p1r.at[l, x, co], p1t.at[ring(x, 4 - x_r), l * 2 + co], at_t1).start()

    @pl.when(jnp.logical_not(away))
    def _():
        p1t[y, h] = p1r[l, x, co]

    ag_p1r = gather_col(p1r)
    next(ag_p1r)
    wide = jnp.concatenate([piece[:RANK], piece[RANK:]], 1)
    cy[y] = lax.dot_general(wide, wcore[...], (((1,), (1,)), ((), ())), precision=lax.Precision.HIGHEST, preferred_element_type=F32)
    m_cy, m_cz, m_cx = new(3), new(3), new(3)
    for d in (2, 1, 3):
        send(m_cy + d - 1, cy.at[y], cy.at[y], at_y(d))

    y_final(1)
    send(m_zf[0, 1], p2.at[y, ring(h, 1), 1], rzf.at[0, 1], at_h(1))

    y_final(2)
    send(m_zf[1, 0], p2.at[y, ring(h, 3), 0], rzf.at[1, 0], at_h(3))
    arrived(m_z1[0], rz1.at[0])
    p2[y, ring(h, 1), 0] += rz1[0]
    send(m_zf[0, 0], p2.at[y, ring(h, 1), 0], rzf.at[0, 0], at_h(1))
    arrived(m_z1[1], rz1.at[1])
    p2[y, ring(h, 3), 1] += rz1[1]
    send(m_zf[1, 1], p2.at[y, ring(h, 3), 1], rzf.at[1, 1], at_h(3))
    y_final(3)
    next(ag_p1r)

    for d in (1, 2, 3):
        arrived(m_cy + d - 1, cy.at[ring(y, 4 - d)])
    cz[h] = cy[0] + cy[1] + cy[2] + cy[3]
    for d in (2, 1, 3):
        send(m_cz + d - 1, cz.at[h], cz.at[h], at_h(d))
    next(ag_p1r)

    for s in (1, 0):
        for side in range(2):
            arrived(m_zf[side, s], rzf.at[side, s])
        p2c[y, h, s] = p2[y, h, s] + rzf[0, s] + rzf[1, s]

    @pl.when(away)
    def _():
        copy(m_t2, p2c.at[y, h], p2r.at[h // 2, ring(y, x), h % 2], at_t2).start()

    @pl.when(jnp.logical_not(away))
    def _():
        p2r[l, x, co] = p2c[y, h]

    ag_p2c = gather_row(p2c)
    next(ag_p2c)

    @pl.when(away)
    def _():
        copy(m_t1, p1t.at[y, h], p1t.at[y, h], at_t2).wait_recv()

    ag_p1t = gather_row(p1t)
    next(ag_p1t)
    next(ag_p1r)
    for d in (1, 2, 3):
        arrived(m_cz + d - 1, cz.at[ring(h, 4 - d)])
    cc[l, x, co] = cz[0] + cz[1] + cz[2] + cz[3]
    for d in (2, 1, 3):
        send(m_cx + d - 1, cc.at[l, x, co], cc.at[l, x, co], at_x(d))
    next(ag_p1r)
    next(ag_p2c)
    @pl.when(away)
    def _():
        copy(m_t2, p2r.at[l, x, co], p2r.at[l, x, co], at_t2).wait_recv()

    ag_p2r = gather_col(p2r)
    next(ag_p2r)
    next(ag_p1t)

    next(ag_p2c)
    next(ag_p1t)
    for d in (1, 2, 3):
        arrived(m_cx + d - 1, cc.at[l, ring(x, 4 - d), co])
    m_cl, m_cc = new(), new()
    send(m_cl, cc.at[l, :, co], cc.at[l, :, co], at_l)
    next(ag_p1t)
    next(ag_p2r)
    next(ag_p2r)
    next(ag_p2c)
    next(ag_p2c)
    next(ag_p1t)
    arrived(m_cl, cc.at[1 - l, :, co])
    send(m_cc, cc.at[:, :, co], cc.at[:, :, co], at_co)
    next(ag_p2r)
    next(ag_p2c)
    next(ag_p1t)
    next(ag_p2r)
    scale = 1.0 / (RANK * RANK)

    def gram(a, b):
        ah, al = split(a.T)
        bh, bl = split(b)
        left = jnp.concatenate([ah, al], 0)
        out = dot(left, bh, ((1,), (0,)))
        return out[:128] + out[128:] + dot(ah, bl, ((1,), (0,)))

    next(ag_p1r)
    next(ag_p1t)
    g = sum(gram(p1r[:, ring(x, d)].reshape(256, 128), p1t[d].reshape(256, 128)) for d in range(4)) * scale
    g1_out[0] = g[:64, :64]
    g1_out[1] = g[64:, 64:]

    arrived(m_cc, cc.at[:, :, 1 - co])
    flat = cc.reshape(16 * RANK, 128)
    for q4 in range(8):
        rows = []
        for j in range(4):
            mine = flat[pl.ds(q4 * 4 + j, 16, stride=RANK), :]
            rows.extend((mine[:, :64], mine[:, 64:]))
        turned = jnp.concatenate(rows, 0).T
        core_out[pl.ds(q4, 64, stride=8), :] = turned
    next(ag_p2r)

    def partial(dy):
        ys = ring(y, dy)
        return [
            gram(
                p2c[ys, :, s].reshape(256, 128),
                p2r[:, ring(ys, x_r), :, s].reshape(256, 128),
            )
            for s in range(2)
        ]

    early = len(sent) - 12
    for idx, src in sent[:early]:
        copy(idx, src, src, at_co).wait_send()
    total = [partial(dy) for dy in (0, 1, 3)]
    next(ag_p2c)
    total.append(partial(2))
    for s in range(2):
        g2_out[s] = sum(t[s] for t in total) * scale

    for idx, src in sent[early:]:
        copy(idx, src, src, at_co).wait_send()

    @pl.when(away)
    def _():
        copy(m_t1, p1r.at[l, x, co], p1r.at[l, x, co], at_t2).wait_send()
        copy(m_t2, p2c.at[y, h], p2c.at[y, h], at_t2).wait_send()

    assert counter[0] <= MESSAGES, counter[0]


MESSAGES = 160


def body(fields, factor_one, factor_two, factor_three):
    vmem = pl.BlockSpec(memory_space=pltpu.VMEM)

    def buf(*shape):
        return pltpu.VMEM((*shape, 128), F32)

    core, g1, g2 = pl.pallas_call(
        kernel,
        out_shape=(
            jax.ShapeDtypeStruct((512, 128), F32),
            jax.ShapeDtypeStruct((2, 64, 64), F32),
            jax.ShapeDtypeStruct((2, 128, 128), F32),
        ),
        in_specs=[pl.BlockSpec(memory_space=pl.ANY), vmem],
        out_specs=(vmem, vmem, vmem),
        scratch_shapes=[
            buf(CHUNKS, 32, 128), buf(4096), buf(4, 4, 2, 64), buf(2, 4, 2, 64), pltpu.VMEM((128, 256), F32),
            buf(2, 4, 64), buf(2, 4, 2, 64), buf(2, 64), buf(2, 2, 64), buf(2, 4, 64), buf(8, 64),
            buf(4, 4, 2, 64), buf(4, 4, 2, 32), buf(2, 4, 2, 2, 64), buf(2, 4, 2, 2, 32),
            buf(4, 32), buf(4, 32), buf(2, 4, 2, 32),
            pltpu.SemaphoreType.DMA((CHUNKS,)),
            pltpu.SemaphoreType.DMA((MESSAGES,)),
            pltpu.SemaphoreType.DMA((MESSAGES,)),
        ],
        compiler_params=pltpu.CompilerParams(
            collective_id=0, has_side_effects=True, vmem_limit_bytes=48 << 20
        ),
        name="tucker",
    )(fields, jnp.concatenate([factor_three.T, factor_two.T, factor_one.T], 1))
    return core.reshape(2, RANK, RANK, RANK), g1, g2


def solution(mesh):
    placed = (P(None, "row", "col", None), P("row", None), P("col", None), P())
    return jax.shard_map(
        body,
        mesh=mesh,
        in_specs=placed,
        out_specs=(P(), P(None, "row", "col"), P(None, "col", "row")),
        check_vma=False,
    )
```

profile of v0, /device:TPU:4, one launch (start us, length us, event | category | flops | bytes accessed | tf_op | source)
XLA Modules:
  0.0 57.6 jit_solution(17889412734611545216)
XLA Ops:
  0.6 0.8 %pad_maximum_fusion.factors = f32[32,320]{1,0:T(8,128)S(1)} fusion(f32[32,64]{1,0:T(8,128)} %bitcast.3, f32[32,128]{1,0:T(8,128)} %bitcast.4, f32[32,128]{1,0:T(8,128)} %bitcast.5), kind=kLoop, calls=%fused_computation | loop fusion | flops 20480 | bytes 81920 | tf_op jit(solution)/shard_map/concatenate | solution.py:486
  1.4 53.7 %tucker.1 = (f32[512,128]{1,0:T(8,128)S(1)}, f32[2,64,64]{2,1,0:T(8,128)S(1)}, f32[2,128,128]{2,1,0:T(8,128)S(1)}) custom-call(f32[2,64,128,128]{3,2,1,0:T(8,128)} %fields.1, f32[32,320]{1,0:T(8,128)S(1)} %pad_maximum_fusion.factors), custom_call_target="tpu_custom_call" | custom-call | tf_op jit(solution)/shard_map/tucker/pallas_call | solution.py:464
  55.1 1.2 %reshape.9 = f32[2,32,32,32]{3,2,1,0:T(8,128)} reshape(f32[512,128]{1,0:T(8,128)S(1)} %get-tuple-element.6) | data formatting | bytes 524288 | tf_op jit(solution)/shard_map/reshape | solution.py:487
  56.3 0.6 %copy.9 = f32[2,64,64]{2,1,0:T(8,128)} copy(f32[2,64,64]{2,1,0:T(8,128)S(1)} %get-tuple-element.13) | data formatting | bytes 65536
  56.9 0.7 %copy.10 = f32[2,128,128]{2,1,0:T(8,128)} copy(f32[2,128,128]{2,1,0:T(8,128)S(1)} %get-tuple-element.14) | data formatting | bytes 262144
where the time goes:
time: 58.4 us; the launch traced here: 57.6 us
  Pallas kernels  53.7 us (92%)
  local copies, waits for them, and re-layouts  2.52 us (4%)
  other arithmetic  0.76 us (1%)
  between operations  0.64 us (1%)
    pallas_call x1, Pallas kernels, body(): pl.pallas_call(kernel, out_shape=(jax.ShapeDtypeStruct((512, 128), F32),...  53.7 us
    unnamed x2, local copies, waits for them, and re-layouts  1.28 us
    reshape x1, local copies, waits for them, and re-layouts, body(): return (core.reshape(2, RANK, RANK, RANK), g1, g2)  1.24 us

commit v1 on v0

--- a/solution.py
+++ b/solution.py
@@ -233,7 +233,7 @@
             arrived(my[dh] + 3, got.at[1])
         yield
 
-    def gather_col(buf):
+    def gather_col(buf, direct=(False, True)):
         ml = new()
         mx = [new(4), new(4)]
         mc = new(8)
@@ -242,7 +242,7 @@
             mine = buf.at[lk, x, co]
             send(mx[k], mine, mine, at_x(1))
             send(mx[k] + 1, mine, mine, at_x(3))
-            if k:
+            if direct[k]:
                 send(mx[k] + 2, mine, mine, at_x(2))
 
         def to_co(lk, k, dx):
@@ -252,12 +252,12 @@
         def x_step(lk, k):
             got = buf.at[lk, ring(x, 3), co]
             arrived(mx[k], got)
-            if not k:
+            if not direct[k]:
                 send(mx[k] + 2, got.at[0], got.at[0], at_x(1))
             to_co(lk, k, 3)
             got = buf.at[lk, ring(x, 1), co]
             arrived(mx[k] + 1, got)
-            if not k:
+            if not direct[k]:
                 send(mx[k] + 3, got.at[1], got.at[1], at_x(3))
             to_co(lk, k, 1)
 
@@ -276,7 +276,7 @@
         yield
         for k, lk in enumerate((l, 1 - l)):
             got = buf.at[lk, ring(x, 2), co]
-            if k:
+            if direct[k]:
                 arrived(mx[k] + 2, got)
             else:
                 arrived(mx[k] + 2, got.at[0])
@@ -311,7 +311,7 @@
     def _():
         p1t[y, h] = p1r[l, x, co]
 
-    ag_p1r = gather_col(p1r)
+    ag_p1r = gather_col(p1r, (False, False))
     next(ag_p1r)
     wide = jnp.concatenate([piece[:RANK], piece[RANK:]], 1)
     cy[y] = lax.dot_general(wide, wcore[...], (((1,), (1,)), ((), ())), precision=lax.Precision.HIGHEST, preferred_element_type=F32)

time: 58.4 us -> 58.4 us (level)
  no operation moved by 1% of the time
where the time goes in v1:
time: 58.4 us; the launch traced here: 57.6 us
  Pallas kernels  53.7 us (92%)
  local copies, waits for them, and re-layouts  2.52 us (4%)
  other arithmetic  0.76 us (1%)
  between operations  0.64 us (1%)
    pallas_call x1, Pallas kernels, body(): pl.pallas_call(kernel, out_shape=(jax.ShapeDtypeStruct((512, 128), F32),...  53.7 us
    unnamed x2, local copies, waits for them, and re-layouts  1.28 us
    reshape x1, local copies, waits for them, and re-layouts, body(): return (core.reshape(2, RANK, RANK, RANK), g1, g2)  1.24 us

profile of v1, /device:TPU:4, one launch (start us, length us, event | category | flops | bytes accessed | tf_op | source)
XLA Modules:
  0.0 57.6 jit_solution(10728316169384376274)
XLA Ops:
  0.6 0.8 %pad_maximum_fusion.factors = f32[32,320]{1,0:T(8,128)S(1)} fusion(f32[32,64]{1,0:T(8,128)} %bitcast.3, f32[32,128]{1,0:T(8,128)} %bitcast.4, f32[32,128]{1,0:T(8,128)} %bitcast.5), kind=kLoop, calls=%fused_computation | loop fusion | flops 20480 | bytes 81920 | tf_op jit(solution)/shard_map/concatenate | solution.py:486
  1.4 53.7 %tucker.1 = (f32[512,128]{1,0:T(8,128)S(1)}, f32[2,64,64]{2,1,0:T(8,128)S(1)}, f32[2,128,128]{2,1,0:T(8,128)S(1)}) custom-call(f32[2,64,128,128]{3,2,1,0:T(8,128)} %fields.1, f32[32,320]{1,0:T(8,128)S(1)} %pad_maximum_fusion.factors), custom_call_target="tpu_custom_call" | custom-call | tf_op jit(solution)/shard_map/tucker/pallas_call | solution.py:464
  55.1 1.2 %reshape.9 = f32[2,32,32,32]{3,2,1,0:T(8,128)} reshape(f32[512,128]{1,0:T(8,128)S(1)} %get-tuple-element.6) | data formatting | bytes 524288 | tf_op jit(solution)/shard_map/reshape | solution.py:487
  56.3 0.6 %copy.9 = f32[2,64,64]{2,1,0:T(8,128)} copy(f32[2,64,64]{2,1,0:T(8,128)S(1)} %get-tuple-element.13) | data formatting | bytes 65536
  56.9 0.7 %copy.10 = f32[2,128,128]{2,1,0:T(8,128)} copy(f32[2,128,128]{2,1,0:T(8,128)S(1)} %get-tuple-element.14) | data formatting | bytes 262144
